TPU v7x, 32 devices: a whole 2x2x4 slice. The times are simulated.
32 devices in a mesh: parts: 2 (over x), leaf: 16 (over z, y, core).
Axes of the slice: x: 2, y: 2, z: 4, core: 2. Of those that a mesh axis runs over, the one named last changes fastest.
Arguments:
- charges: bfloat16 [1024, 64, 128], P(('parts', 'leaf')), parts along dimension 0, may hold values from -6 to 6
- near_blocks: bfloat16 [1024, 8, 128, 128], P(('parts', 'leaf')), parts along dimension 0, may hold values from -0.1875 to 0.1875
- near_index: int32 [1024, 8], P(('parts', 'leaf')), parts along dimension 0, may hold values from 0 to 511, as said below
- near_count: int32 [1024], P(('parts', 'leaf')), parts along dimension 0, may hold values from 1 to 8
- leaf_basis: bfloat16 [1024, 64, 128], P(('parts', 'leaf')), parts along dimension 0, may hold values from -0.5 to 0.5
- leaf_coupling: bfloat16 [1024, 8, 64, 64], P(('parts', 'leaf')), parts along dimension 0, may hold values from -0.25 to 0.25
- far_index: int32 [1024, 8], P(('parts', 'leaf')), parts along dimension 0, may hold values from 0 to 511, as said below
- transfer: bfloat16 [1024, 64, 64], P(('parts', 'leaf')), parts along dimension 0, may hold values from -0.75 to 0.75
- cluster_coupling: bfloat16 [32, 16, 64, 64], P(('parts', 'leaf')), parts along dimension 0, may hold values from -0.03125 to 0.03125
- cluster_index: int32 [32, 16], P(('parts', 'leaf')), parts along dimension 0, may hold values from 0 to 15, as said below
Outputs:
- potential: bfloat16 [1024, 64, 128], P(('parts', 'leaf')), parts along dimension 0
There are 2 independent parts, one for each index of `parts`. A program takes and returns all parts, laid end to end along the dimension named above; each array names one. Nothing has to cross between parts.
Inputs may be any that keep to these rules, and one draw needn't show every extreme that they name: `near_index`: every entry is within 32 leaves of its own leaf, counted cyclically; slot 0 is the leaf itself; slots at or past near_count hold some valid leaf. `far_index`: every entry is within 32 leaves of its own leaf, counted cyclically. `cluster_index`: every entry is within 7 clusters of its own cluster, counted cyclically; entry 0 lies exactly 7 below and entry 1 exactly 7 above.
All inputs are finite; a program needn't handle non-finite values.
Results may differ from a plain program's by a relative error of at most 0.0054.
Values may be sent and summed in bfloat16 or wider, within the bound.
A program may use at most 128 MiB of HBM per device.

v0:
```python
import jax
import jax.numpy as jnp
from jax import lax
from jax.sharding import PartitionSpec as P


def padded(cells, sides, width):
    for axis, dim in sides:
        count = lax.axis_size(axis)
        head = lax.slice_in_dim(cells, 0, width, axis=dim)
        tail = lax.slice_in_dim(cells, cells.shape[dim] - width, cells.shape[dim], axis=dim)
        cells = jnp.concatenate(
            [
                lax.ppermute(tail, axis, [(i, (i + 1) % count) for i in range(count)]),
                cells,
                lax.ppermute(head, axis, [((i + 1) % count, i) for i in range(count)]),
            ],
            axis=dim,
        )
    return cells


def shards(
    charges,
    near_blocks,
    near_index,
    near_count,
    leaf_basis,
    leaf_coupling,
    far_index,
    transfer,
    cluster_coupling,
    cluster_index,
):
    high = lax.Precision.HIGHEST
    leaves_dev = charges.shape[0]
    devices = lax.axis_size("leaf")
    total = leaves_dev * devices
    first_leaf = lax.axis_index("leaf") * leaves_dev
    padded_charges = padded(charges, (("leaf", 0),), leaves_dev)
    moments = jnp.einsum(
        "irp,ikp->irk", charges, leaf_basis, preferred_element_type=jnp.float32
    ).astype(jnp.bfloat16)
    padded_moments = padded(moments, (("leaf", 0),), leaves_dev)
    near_pos = (near_index - first_leaf + leaves_dev) % total
    far_pos = (far_index - first_leaf + leaves_dev) % total
    lifted = jnp.einsum("irk,ick->rc", moments, transfer, preferred_element_type=jnp.float32)
    own_list = cluster_index[0]
    own_coupling = cluster_coupling[0].astype(jnp.float32)
    every = lax.all_gather(lifted[None], "leaf", axis=0, tiled=True)
    picked = every[own_list]
    cluster_local = jnp.einsum("frk,ftk->rt", picked, own_coupling, precision=high)
    far_moments = padded_moments[far_pos]
    leaf_far = jnp.einsum(
        "ifrk,iftk->irt", far_moments, leaf_coupling, preferred_element_type=jnp.float32
    )
    downward = jnp.einsum(
        "rc,ick->irk", cluster_local, transfer.astype(jnp.float32), precision=high
    )
    leaf_local = (leaf_far + downward).astype(jnp.bfloat16)
    gathered = padded_charges[near_pos]
    used = (jnp.arange(near_pos.shape[1])[None, :] < near_count[:, None])[:, :, None, None]
    gathered = jnp.where(used, gathered, jnp.zeros((), jnp.bfloat16))
    near_sum = jnp.einsum(
        "isrp,istp->irt", gathered, near_blocks, preferred_element_type=jnp.float32
    )
    far_part = jnp.einsum(
        "irk,ikp->irp", leaf_local, leaf_basis, preferred_element_type=jnp.float32
    )
    return (far_part + near_sum).astype(jnp.bfloat16)


def solution(mesh):
    placed = (
        P(("parts", "leaf"), None, None),
        P(("parts", "leaf"), None, None, None),
        P(("parts", "leaf"), None),
        P(("parts", "leaf")),
        P(("parts", "leaf"), None, None),
        P(("parts", "leaf"), None, None, None),
        P(("parts", "leaf"), None),
        P(("parts", "leaf"), None, None),
        P(("parts", "leaf"), None, None, None),
        P(("parts", "leaf"), None),
    )
    return jax.shard_map(
        shards,
        mesh=mesh,
        in_specs=placed,
        out_specs=P(("parts", "leaf"), None, None),
        check_vma=False,
    )
```

profile of v0, /device:TPU:1, one launch (start us, length us, event | category | flops | bytes accessed | tf_op | source)
XLA Modules:
  0.0 71.6 jit_solution(14136548286489401449)
XLA Ops:
  0.0 1.1 %copy-done = bf16[32,64,128]{2,1,0:T(8,128)(2,1)S(1)} copy-done((bf16[32,64,128]{2,1,0:T(8,128)(2,1)S(1)}, bf16[32,64,128]{2,1,0:T(8,128)(2,1)}, u32[]{:S(2)}) %copy-start) | copy-done | bytes 524312
  1.1 1.4 %convolution_convert_fusion = bf16[32,64,64]{2,1,0:T(8,128)(2,1)S(1)} fusion(bf16[32,64,128]{2,1,0:T(8,128)(2,1)} %param.10, bf16[32,64,128]{2,1,0:T(8,128)(2,1)S(1)} %copy-done), kind=kOutput, calls=%fused_computation.16 | convolution fusion | flops 33685504 | bytes 1310720 | tf_op jit(solution)/shard_map/irp,ikp->irk/dot_general | solution.py:41
  2.6 2.7 %collective-permute-start = (bf16[32,64,64]{2,1,0:T(8,128)(2,1)S(1)}, bf16[32,64,64]{2,1,0:T(8,128)(2,1)}, u32[]{:S(2)}, u32[]{:S(2)}) collective-permute-start(bf16[32,64,64]{2,1,0:T(8,128)(2,1)S(1)} %convolution_convert_fusion), channel_id=1, source_target_pairs={{0,1},{1,2},{2,3},{3,4},{4,5},{5,6},{6,7},{7,8},{8,9},{9,10},{10,1... | collective-permute-start | bytes 786440 | tf_op jit(solution)/shard_map/ppermute | solution.py:14
  5.2 1.7 %collective-permute-start.2 = (bf16[32,64,128]{2,1,0:T(8,128)(2,1)}, bf16[32,64,128]{2,1,0:T(8,128)(2,1)S(1)}, u32[]{:S(2)}, u32[]{:S(2)}) collective-permute-start(bf16[32,64,128]{2,1,0:T(8,128)(2,1)} %param.10), channel_id=1, source_target_pairs={{0,1},{1,2},{2,3},{3,4},{4,5},{5,6},{6,7},{7,8},{8,9},{9,10},{10,1... | collective-permute-start | bytes 1572872 | tf_op jit(solution)/shard_map/ppermute | solution.py:14
  7.0 1.2 %collective-permute-start.3 = (bf16[32,64,128]{2,1,0:T(8,128)(2,1)}, bf16[32,64,128]{2,1,0:T(8,128)(2,1)}, u32[]{:S(2)}, u32[]{:S(2)}) collective-permute-start(bf16[32,64,128]{2,1,0:T(8,128)(2,1)} %param.10), channel_id=1, source_target_pairs={{1,0},{2,1},{3,2},{4,3},{5,4},{6,5},{7,6},{8,7},{9,8},{10,9},{11,1... | collective-permute-start | bytes 1572872 | tf_op jit(solution)/shard_map/ppermute | solution.py:16
  8.2 0.7 compare_select_fusion
  8.9 0.1 copy.11
  9.0 0.1 reshape.51
  9.1 1.3 %convolution_bitcast_fusion.2 = f32[64,64]{1,0:T(8,128)S(1)} fusion(bf16[32,64,64]{2,1,0:T(8,128)(2,1)S(1)} %convolution_convert_fusion, bf16[32,64,64]{2,1,0:T(8,128)(2,1)} %param.17), kind=kOutput, calls=%fused_computation.18 | convolution fusion | flops 16777216 | bytes 540672 | tf_op jit(solution)/shard_map/irk,ick->rc/dot_general | solution.py:47
  10.4 33.4 %all-gather = f32[1024,64]{1,0:T(8,128)S(1)} all-gather(f32[64,64]{1,0:T(8,128)S(1)} %convolution_bitcast_fusion.2), channel_id=2, replica_groups=mesh['parts'=2,'leaf'=16] {'leaf'}, dimensions={0}, use_global_device_ids=true | all-gather | bytes 278528 | tf_op jit(solution)/shard_map/all_gather | solution.py:50
  43.9 0.7 fusion.20
  44.5 0.1 copy.12
  44.6 0.1 reshape.67
  44.7 0.7 %iota_compare_fusion = pred[32,8]{1,0:T(8,128)(4,1)S(1)} fusion(s32[32]{0:T(128)} %param.13), kind=kLoop, calls=%fused_computation.21 | loop fusion | flops 256 | bytes 384 | tf_op jit(solution)/shard_map/lt | solution.py:62
  45.4 0.6 gather_fusion.1
  46.0 0.4 fusion.16
  46.4 1.5 %convolution_bitcast_fusion = f32[32,64,64]{2,1,0:T(8,128)} fusion(f32[64,64,1]{1,0,2:T(8,128)S(1)} %fusion.16, bf16[32,64,64]{2,1,0:T(8,128)(2,1)S(1)} %copy-done.1), kind=kOutput, calls=%fused_computation.9 | convolution fusion | flops 100663296 | bytes 802816 | tf_op jit(solution)/shard_map/rc,ick->irk/dot_general | solution.py:57
  47.9 0.0 collective-permute-done
  48.0 1.5 %pad_maximum_fusion = bf16[96,64,64]{2,1,0:T(8,128)(2,1)S(1)} fusion(bf16[32,64,64]{2,1,0:T(8,128)(2,1)} %collective-permute-done.1, bf16[32,64,64]{2,1,0:T(8,128)(2,1)S(1)} %convolution_convert_fusion, bf16[32,64,64]{2,1,0:T(8,128)(2,1)} %collective-permute-done), kind=kLoop, calls=%fused_computation.7 | loop fusion | flops 786432 | bytes 1572864 | tf_op jit(solution)/shard_map/concatenate | solution.py:12
  49.5 3.0 %gather_fusion = bf16[256,64,64]{2,1,0:T(8,128)(2,1)} fusion(bf16[96,64,64]{2,1,0:T(8,128)(2,1)S(1)} %pad_maximum_fusion, s32[1024]{0:T(1024)S(1)} %pad_clamp_fusion.2), kind=kCustom, calls=%fused_computation | custom fusion | bytes 4195328 | tf_op jit(solution)/shard_map/gather | solution.py:53
  52.5 6.1 %fusion.15 = f32[32,64,128]{2,1,0:T(8,128)} fusion(bf16[32,64,128]{2,1,0:T(8,128)(2,1)S(1)} %copy-done, f32[32,64,64]{2,1,0:T(8,128)} %convolution_bitcast_fusion, bf16[32,8,64,64]{3,2,1,0:T(8,128)(2,1)} %bitcast.42, bf16[32,8,64,64]{3,2,1,0:T(8,128)(2,1)} %param.15), kind=kOutput, calls=%fused_computation.17 | convolution fusion | flops 168034304 | bytes 6291456 | tf_op jit(solution)/shard_map/irk,ikp->irp/dot_general | solution.py:67
  58.7 1.2 %pad_maximum_fusion.1 = bf16[96,64,128]{2,1,0:T(8,128)(2,1)S(1)} fusion(bf16[32,64,128]{2,1,0:T(8,128)(2,1)} %collective-permute-done.3, bf16[32,64,128]{2,1,0:T(8,128)(2,1)S(1)} %copy-done.2, bf16[32,64,128]{2,1,0:T(8,128)(2,1)S(1)} %collective-permute-done.2), kind=kLoop, calls=%fused_computation.8 | loop fusion | flops 1572864 | bytes 3145728 | tf_op jit(solution)/shard_map/concatenate | solution.py:12
  59.9 3.0 %gather_fusion.2 = bf16[256,64,128]{2,1,0:T(8,128)(2,1)} fusion(bf16[96,64,128]{2,1,0:T(8,128)(2,1)S(1)} %pad_maximum_fusion.1, s32[1024]{0:T(1024)S(1)} %pad_clamp_fusion), kind=kCustom, calls=%fused_computation.2 | custom fusion | bytes 8389632 | tf_op jit(solution)/shard_map/gather | solution.py:61
  62.9 8.7 %fusion.12 = bf16[32,64,128]{2,1,0:T(8,128)(2,1)} fusion(f32[32,64,128]{2,1,0:T(8,128)} %fusion.15, bf16[32,8,128,128]{3,2,1,0:T(8,128)(2,1)} %param.11, bf16[32,8,64,128]{3,2,1,0:T(8,128)(2,1)} %bitcast.43, pred[32,8]{1,0:T(8,128)(4,1)S(1)} %iota_compare_fusion), kind=kOutput, calls=%fused_computation.15 | convolution fusion | flops 539492352 | bytes 14156032 | tf_op jit(solution)/shard_map/isrp,istp->irt/dot_general | solution.py:64
  (14 shorter events, 0.0 us)
Async XLA Ops:
  0.0 1.1 %copy-start = (bf16[32,64,128]{2,1,0:T(8,128)(2,1)S(1)}, bf16[32,64,128]{2,1,0:T(8,128)(2,1)}, u32[]{:S(2)}) copy-start(bf16[32,64,128]{2,1,0:T(8,128)(2,1)} %param.14) | copy-start | bytes 1572868
  0.0 46.4 %copy-start.1 = (bf16[32,64,64]{2,1,0:T(8,128)(2,1)S(1)}, bf16[32,64,64]{2,1,0:T(8,128)(2,1)}, u32[]{:S(2)}) copy-start(bf16[32,64,64]{2,1,0:T(8,128)(2,1)} %param.17) | copy-start | bytes 786436
  0.0 46.0 %copy-start.3 = (bf16[1,16,64,64]{3,2,1,0:T(8,128)(2,1)S(1)}, bf16[1,16,64,64]{3,2,1,0:T(8,128)(2,1)}, u32[]{:S(2)}) copy-start(bf16[1,16,64,64]{3,2,1,0:T(8,128)(2,1)} %param.18) | copy-start | bytes 393220
  2.6 45.4 %collective-permute-start = (bf16[32,64,64]{2,1,0:T(8,128)(2,1)S(1)}, bf16[32,64,64]{2,1,0:T(8,128)(2,1)}, u32[]{:S(2)}, u32[]{:S(2)}) collective-permute-start(bf16[32,64,64]{2,1,0:T(8,128)(2,1)S(1)} %convolution_convert_fusion), channel_id=1, source_target_pairs={{0,1},{1,2},{2,3},{3,4},{4,5},{5,6},{6,7},{7,8},{8,9},{9,10},{10,1... | collective-permute-start | bytes 786440 | tf_op jit(solution)/shard_map/ppermute | solution.py:14
  5.2 42.7 %collective-permute-start.1 = (bf16[32,64,64]{2,1,0:T(8,128)(2,1)S(1)}, bf16[32,64,64]{2,1,0:T(8,128)(2,1)}, u32[]{:S(2)}, u32[]{:S(2)}) collective-permute-start(bf16[32,64,64]{2,1,0:T(8,128)(2,1)S(1)} %convolution_convert_fusion), channel_id=1, source_target_pairs={{1,0},{2,1},{3,2},{4,3},{5,4},{6,5},{7,6},{8,7},{9,8},{10,9},{11,1... | collective-permute-start | bytes 786440 | tf_op jit(solution)/shard_map/ppermute | solution.py:16
  5.2 53.4 %collective-permute-start.2 = (bf16[32,64,128]{2,1,0:T(8,128)(2,1)}, bf16[32,64,128]{2,1,0:T(8,128)(2,1)S(1)}, u32[]{:S(2)}, u32[]{:S(2)}) collective-permute-start(bf16[32,64,128]{2,1,0:T(8,128)(2,1)} %param.10), channel_id=1, source_target_pairs={{0,1},{1,2},{2,3},{3,4},{4,5},{5,6},{6,7},{7,8},{8,9},{9,10},{10,1... | collective-permute-start | bytes 1572872 | tf_op jit(solution)/shard_map/ppermute | solution.py:14
  7.0 51.7 %collective-permute-start.3 = (bf16[32,64,128]{2,1,0:T(8,128)(2,1)}, bf16[32,64,128]{2,1,0:T(8,128)(2,1)}, u32[]{:S(2)}, u32[]{:S(2)}) collective-permute-start(bf16[32,64,128]{2,1,0:T(8,128)(2,1)} %param.10), channel_id=1, source_target_pairs={{1,0},{2,1},{3,2},{4,3},{5,4},{6,5},{7,6},{8,7},{9,8},{10,9},{11,1... | collective-permute-start | bytes 1572872 | tf_op jit(solution)/shard_map/ppermute | solution.py:16
  52.5 6.1 %copy-start.2 = (bf16[32,64,128]{2,1,0:T(8,128)(2,1)S(1)}, bf16[32,64,128]{2,1,0:T(8,128)(2,1)}, u32[]{:S(2)}) copy-start(bf16[32,64,128]{2,1,0:T(8,128)(2,1)} %param.10) | copy-start | bytes 1572868
where the time goes:
time: 72.2 us; the launch traced here: 71.6 us
  blocking collectives  33.4 us (46%)
  matrix products  19.5 us (27%)
  local copies, waits for them, and re-layouts  8.09 us (11%)
  starting transfers between devices  5.62 us (8%)
  other arithmetic  4.89 us (7%)
    all_gather x1, blocking collectives, shards(): every = lax.all_gather(lifted[None], 'leaf', axis=0, tiled=True)  33.4 us
    dot_general x1, matrix products, shards(): jnp.einsum('isrp,istp->irt', gathered, near_blocks, preferred_element_typ...  8.68 us
    dot_general x1, matrix products, shards(): jnp.einsum('irk,ikp->irp', leaf_local, leaf_basis, preferred_element_type...  6.13 us
    ppermute x2, starting transfers between devices, padded(): lax.ppermute(tail, axis, [(i, (i + 1) % count) for i in range(count)])  4.42 us
    gather x1, local copies, waits for them, and re-layouts, shards(): far_moments = padded_moments[far_pos]  3.03 us
    gather x1, local copies, waits for them, and re-layouts, shards(): gathered = padded_charges[near_pos]  3.03 us
    concatenate x2, other arithmetic, padded(): jnp.concatenate([lax.ppermute(tail, axis, [(i, (i + 1) % count) for i in...  2.76 us
    dot_general x1, matrix products, shards(): jnp.einsum('rc,ick->irk', cluster_local, transfer.astype(jnp.float32), pr...  1.51 us
  transfers between devices with their start and end apart: 4, of which 0 were waited for; matrix products, arithmetic and copies ran while one was open for 24% of the time, Pallas kernels for 0%

commit v1 on v0

v1 whole, which is shorter than its diff:
```python
import functools

import jax
import jax.numpy as jnp
from jax import lax
from jax.experimental import pallas as pl
from jax.experimental.pallas import tpu as pltpu
from jax.sharding import PartitionSpec as P

MESH = pl.DeviceIdType.MESH
F32 = jnp.float32
BF16 = jnp.bfloat16


def dot_t(a, b):
    return lax.dot_general(a, b, (((1,), (1,)), ((), ())), preferred_element_type=F32)


def kernel(
    n, reach, chunks, size, early,
    ch, nb, ni, nc, lb, lc, fi, tr, cc, ci, out,
    cst, mst, hslow_c, hslow_m, hfast_m, mpack, tpk, basis, trans, ccv, cmall, cmown, nbuf, cbuf, obuf,
    fc_send, fc_recv, fm_send, fm_recv, sc_send, sc_recv, sm_send, sm_recv, cl_send, cl_recv,
    own_sem, near_sem, coup_sem, out_sem,
):
    leaves = chunks * size
    total = n * leaves
    slots = ni.shape[0]
    farl = fi.shape[0]
    me = lax.axis_index("leaf")
    odd = lax.rem(me, 2)
    even = 1 - odd
    first = me * leaves
    fast = me + 1 - 2 * odd
    slow = lax.rem(me - 1 + 2 * odd + n, n)

    def block(q):
        return q + even * (chunks - 1 - 2 * q)

    def sent(q):
        return q + odd * (chunks - 1 - 2 * q)

    own = [
        pltpu.make_async_copy(ch, cst.at[pl.ds(leaves, leaves)], own_sem.at[0]),
        pltpu.make_async_copy(lb, basis, own_sem.at[1]),
        pltpu.make_async_copy(tr, trans, own_sem.at[2]),
        pltpu.make_async_copy(cc, ccv, own_sem.at[3]),
    ]
    for copy in own:
        copy.start()

    barrier = pltpu.get_barrier_semaphore()
    for o in range(1, reach + 1):
        for d in (o, n - o):
            pl.semaphore_signal(
                barrier, inc=1, device_id={"leaf": lax.rem(me + d, n)}, device_id_type=MESH
            )
    pl.semaphore_wait(barrier, 2 * reach)

    def remote(src, dst, send, recv, d):
        return pltpu.make_async_remote_copy(
            src_ref=src, dst_ref=dst, send_sem=send, recv_sem=recv,
            device_id={"leaf": d}, device_id_type=MESH,
        )

    def slow_c(q):
        return remote(
            ch.at[pl.ds(sent(q) * size, size)], hslow_c.at[q], sc_send.at[q], sc_recv.at[q], slow
        )

    def slow_m(q):
        return remote(mpack.at[sent(q)], hslow_m.at[q], sm_send.at[q], sm_recv.at[q], slow)

    fast_c = remote(
        ch, cst.at[pl.ds(odd * (2 * leaves), leaves)], fc_send.at[0], fc_recv.at[0], fast
    )
    fast_m = remote(mpack, hfast_m, fm_send.at[0], fm_recv.at[0], fast)

    def near_copy(q):
        return pltpu.make_async_copy(
            nb.at[pl.ds(block(q) * size, size)], nbuf.at[q], near_sem.at[q]
        )

    def coup_copy(q):
        return pltpu.make_async_copy(
            lc.at[pl.ds(block(q) * size, size)], cbuf.at[q], coup_sem.at[q]
        )

    def out_copy(q):
        return pltpu.make_async_copy(
            obuf.at[q], out.at[pl.ds(block(q) * size, size)], out_sem.at[q]
        )

    def loop(lo, hi, body):
        def step(i, c):
            body(i)
            return c
        lax.fori_loop(lo, hi, step, 0)

    loop(0, early, lambda q: slow_c(q).start())
    fast_c.start()
    cst[3 * leaves] = jnp.zeros(cst.shape[1:], BF16)
    for copy in own[:3]:
        copy.wait()

    left = lax.broadcasted_iota(jnp.int32, (ch.shape[1], 128), 1) < 64

    def lift_step(b, lift):
        for j in range(size // 2):
            both = []
            for h in range(2):
                leaf = b * size + 2 * j + h
                twice = jnp.concatenate([basis[leaf], basis[leaf]], axis=0)
                m = dot_t(cst[leaves + leaf], twice)
                mst[leaves + leaf] = m.astype(BF16)
                both.append(m)
            packed = jnp.where(left, both[0], both[1]).astype(BF16)
            mpack[b, j] = packed
            pair = jnp.concatenate(
                [trans[b * size + 2 * j], trans[b * size + 2 * j + 1]], axis=1
            )
            tpk[b, j] = pair
            lift = lift + dot_t(packed, pair)
        return lift

    rank = lb.shape[1]
    lift = lax.fori_loop(0, chunks, lift_step, jnp.zeros((ch.shape[1], rank), F32))
    half = lift.shape[0] // 2
    lifted = jnp.concatenate([lift[:half], lift[half:]], axis=1).astype(BF16)
    cmown[...] = lifted
    cmall[reach] = lifted

    def cluster(o):
        at = 0 if o < 0 else 1
        i = 2 * (abs(o) - 1) + at
        j = 2 * (abs(o) - 1) + at
        return remote(
            cmown, cmall.at[reach - o], cl_send.at[i], cl_recv.at[j], lax.rem(me + o + n, n)
        )

    offsets = [s * o for o in range(reach, 0, -1) for s in (1, -1)]
    for o in offsets:
        cluster(o).start()
    fast_m.start()

    def rest(q):
        slow_m(q).start()
        slow_c(q + early).start()

    loop(0, chunks - early, rest)
    loop(chunks - early, chunks, lambda q: slow_m(q).start())

    def fetch(q):
        near_copy(q).start()
        coup_copy(q).start()

    loop(0, chunks, fetch)

    def spread(packed, at):
        a = packed[:, :64]
        b = packed[:, 64:]
        mst[at] = jnp.concatenate([a, a], axis=1)
        mst[at + 1] = jnp.concatenate([b, b], axis=1)

    fast_c.wait_recv()
    fast_m.wait_recv()
    fast_base = even * (2 * leaves)
    slow_base = odd * (2 * leaves)

    def unpack_fast(b):
        for j in range(size // 2):
            spread(hfast_m[b, j], fast_base + b * size + 2 * j)

    loop(0, chunks, unpack_fast)

    own[3].wait()
    for o in offsets:
        cluster(o).wait_recv()
    local = jnp.zeros((ch.shape[1], rank), F32)
    for f in range(ci.shape[1]):
        slot = jnp.clip(lax.rem(ci[0, f] - me + reach + n, n), 0, 2 * reach)
        p = cmall[slot]
        picked = jnp.concatenate([p[:, :64], p[:, 64:]], axis=0)
        local = local + dot_t(picked, ccv[0, f])
    local = local.astype(BF16)

    def work(q):
        slow_c(q).wait_recv()
        slow_m(q).wait_recv()
        near_copy(q).wait()
        coup_copy(q).wait()
        b = block(q)
        cst[pl.ds(slow_base + b * size, size)] = hslow_c[q]
        for j in range(size // 2):
            spread(hslow_m[q, j], slow_base + b * size + 2 * j)

        def place(index):
            return jnp.clip(lax.rem(index - first + leaves + total, total), 0, 3 * leaves - 1)

        for j in range(size // 2):
            down = jnp.dot(local, tpk[b, j], preferred_element_type=F32)
            for h in range(2):
                at = 2 * j + h
                leaf = b * size + at
                count = nc[leaf]
                lhs, rhs = [], []
                for s in range(slots):
                    pos = jnp.where(s < count, place(ni[s, leaf]), 3 * leaves)
                    lhs.append(cst[pos])
                    rhs.append(nbuf[q, at, s])
                near = dot_t(jnp.concatenate(lhs, axis=1), jnp.concatenate(rhs, axis=1))
                lhs, rhs = [], []
                for f in range(0, farl, 2):
                    lhs.append(
                        jnp.where(left, mst[place(fi[f, leaf])], mst[place(fi[f + 1, leaf])])
                    )
                    rhs.append(
                        jnp.concatenate([cbuf[q, at, f], cbuf[q, at, f + 1]], axis=1)
                    )
                far = dot_t(jnp.concatenate(lhs, axis=1), jnp.concatenate(rhs, axis=1))
                ll = (far + down[:, h * 64 : h * 64 + 64]).astype(BF16)
                far_part = jnp.dot(ll, basis[leaf], preferred_element_type=F32)
                obuf[q, at] = (near + far_part).astype(BF16)
        out_copy(q).start()

    loop(0, chunks, work)

    def finish(q):
        out_copy(q).wait()
        slow_c(q).wait_send()
        slow_m(q).wait_send()

    loop(0, chunks, finish)
    fast_c.wait_send()
    fast_m.wait_send()
    for o in offsets:
        cluster(o).wait_send()


def shards(n, charges, near_blocks, near_index, near_count, leaf_basis, leaf_coupling,
           far_index, transfer, cluster_coupling, cluster_index):
    leaves, rhs, points = charges.shape
    rank = leaf_basis.shape[1]
    size = 4
    chunks = leaves // size
    early = 2
    reach = min(16, (n - 1) // 2)
    hbm = pl.BlockSpec(memory_space=pl.ANY)
    smem = pl.BlockSpec(memory_space=pltpu.SMEM)
    dma = pltpu.SemaphoreType.DMA
    packed = (chunks, size // 2, rhs, 2 * rank)
    return pl.pallas_call(
        functools.partial(kernel, n, reach, chunks, size, early),
        out_shape=jax.ShapeDtypeStruct(charges.shape, BF16),
        in_specs=[hbm, hbm, smem, smem, hbm, hbm, smem, hbm, hbm, smem],
        out_specs=hbm,
        scratch_shapes=[
            pltpu.VMEM((3 * leaves + 1, rhs, points), BF16),
            pltpu.VMEM((3 * leaves, rhs, 2 * rank), BF16),
            pltpu.VMEM((chunks, size, rhs, points), BF16),
            pltpu.VMEM(packed, BF16),
            pltpu.VMEM(packed, BF16),
            pltpu.VMEM(packed, BF16),
            pltpu.VMEM((chunks, size // 2, rank, 2 * rank), BF16),
            pltpu.VMEM(leaf_basis.shape, BF16),
            pltpu.VMEM(transfer.shape, BF16),
            pltpu.VMEM(cluster_coupling.shape, BF16),
            pltpu.VMEM((2 * reach + 1, rhs // 2, 2 * rank), BF16),
            pltpu.VMEM((rhs // 2, 2 * rank), BF16),
            pltpu.VMEM((chunks, size) + near_blocks.shape[1:], BF16),
            pltpu.VMEM((chunks, size) + leaf_coupling.shape[1:], BF16),
            pltpu.VMEM((chunks, size, rhs, points), BF16),
            dma((1,)), dma((1,)), dma((1,)), dma((1,)),
            dma((chunks,)), dma((chunks,)), dma((chunks,)), dma((chunks,)),
            dma((2 * reach,)), dma((2 * reach,)),
            dma((4,)), dma((chunks,)), dma((chunks,)), dma((chunks,)),
        ],
        compiler_params=pltpu.CompilerParams(
            collective_id=0, has_side_effects=True, vmem_limit_bytes=60 * 1024 * 1024
        ),
    )(charges, near_blocks, near_index.T, near_count, leaf_basis, leaf_coupling,
      far_index.T, transfer, cluster_coupling, cluster_index)


def solution(mesh):
    three = P(("parts", "leaf"), None, None)
    four = P(("parts", "leaf"), None, None, None)
    two = P(("parts", "leaf"), None)
    placed = (three, four, two, P(("parts", "leaf")), three, four, two, three, four, two)
    return jax.shard_map(
        functools.partial(shards, mesh.shape["leaf"]),
        mesh=mesh,
        in_specs=placed,
        out_specs=three,
        check_vma=False,
    )
```

time: 72.2 us -> 32.7 us (0.45)
  blocking collectives: 33.4 us -> 0 us
  Pallas kernels: 0 us -> 30.6 us
  matrix products: 19.5 us -> 0 us
  local copies, waits for them, and re-layouts: 8.09 us -> 1.87 us
  starting transfers between devices: 5.62 us -> 0 us
  other arithmetic: 4.89 us -> 0 us
    all_gather x1 -> x0, blocking collectives: 33.4 us -> none  [shards(): every = lax.all_gather(lifted[None], 'leaf', axis=0, tiled=True)]
    pallas_call x0 -> x1, Pallas kernels: none -> 30.6 us  [shards(): pl.pallas_call(functools.partial(kernel, n, reach, chunks, size, early),...]
    dot_general x6 -> x0, matrix products: 19.5 us -> none  [the longest x1 8.68 us: shards(): jnp.einsum('isrp,istp->irt', gathered, near_blocks, preferred_element_typ...]
    gather x3 -> x0, local copies, waits for them, and re-layouts: 6.64 us -> none  [the longest x1 3.03 us: shards(): far_moments = padded_moments[far_pos]]
    ppermute x4 -> x0, starting transfers between devices: 5.62 us -> none  [the longest x2 4.42 us: padded(): lax.ppermute(tail, axis, [(i, (i + 1) % count) for i in range(count)])]
    concatenate x2 -> x0, other arithmetic: 2.76 us -> none  [padded(): jnp.concatenate([lax.ppermute(tail, axis, [(i, (i + 1) % count) for i in...]
    select_n x2 -> x0, other arithmetic: 1.37 us -> none  [the longest x1 0.72 us: shards(): gathered = padded_charges[near_pos]]
    unnamed x8 -> x1, local copies, waits for them, and re-layouts: 1.12 us -> 1.87 us
  transfers between devices with their start and end apart: 4 -> 0, of which waited for: 0 -> 0; matrix products, arithmetic and copies ran while one was open for 24% -> 0% of each run, Pallas kernels for 0% -> 0%
where the time goes in v1:
time: 32.7 us; the launch traced here: 32.5 us
  Pallas kernels  30.6 us (94%)
  local copies, waits for them, and re-layouts  1.87 us (6%)
    pallas_call x1, Pallas kernels, shards(): pl.pallas_call(functools.partial(kernel, n, reach, chunks, size, early),...  30.6 us
    unnamed x1, local copies, waits for them, and re-layouts  1.87 us

profile of v1, /device:TPU:1, one launch (start us, length us, event | category | flops | bytes accessed | tf_op | source)
XLA Modules:
  0.0 32.5 jit_solution(12160201537672586159)
XLA Ops:
  0.0 30.6 %shard_map.100 = bf16[32,64,128]{2,1,0:T(8,128)(2,1)} custom-call(bf16[32,64,128]{2,1,0:T(8,128)(2,1)} %ch.1, bf16[32,8,128,128]{3,2,1,0:T(8,128)(2,1)} %nb.1, s32[8,32]{1,0:T(8,128)} %bitcast.2, s32[32]{0:T(128)} %nc.1, bf16[32,64,128]{2,1,0:T(8,128)(2,1)} %lb.1, bf16[32,8,64,64]{3,2,1,0:T(8,128)(2,1)} %lc.1, s32[8,32]{1,0:T(8,128)} %bitcast.3, ...), custom_call_target="tpu_custom_call" | custom-call | tf_op jit(solution)/shard_map/pallas_call | solution.py:252
  30.6 1.9 %copy.12 = bf16[32,64,128]{2,1,0:T(8,128)(2,1)} copy(bf16[32,64,128]{2,1,0:T(8,128)(2,1)} %shard_map.100) | data formatting | bytes 1048576

commit v2 on v1

v2 whole, which is shorter than its diff:
```python
import functools

import jax
import jax.numpy as jnp
from jax import lax
from jax.experimental import pallas as pl
from jax.experimental.pallas import tpu as pltpu
from jax.sharding import PartitionSpec as P

MESH = pl.DeviceIdType.MESH
F32 = jnp.float32
BF16 = jnp.bfloat16


def dot_t(a, b):
    return lax.dot_general(a, b, (((1,), (1,)), ((), ())), preferred_element_type=F32)


def kernel(
    n, chunks, size, early, parted,
    ch, nb, ni, nc, lb, lc, fi, tr, cc, ci, out,
    cst, mst, hslow_c, hslow_m, hfast_m, mpack, tpk, basis, trans, ccv, cmall, nbuf, cbuf, nsum, fsum,
    fc_send, fc_recv, fm_send, fm_recv, sc_send, sc_recv, sm_send, sm_recv, cl_send, cl_recv,
    own_sem, near_sem, coup_sem,
):
    leaves = chunks * size
    total = n * leaves
    slots = ni.shape[0]
    farl = fi.shape[0]
    me = lax.axis_index("leaf")
    odd = lax.rem(me, 2)
    even = 1 - odd
    first = me * leaves
    fast = me + 1 - 2 * odd
    slow = lax.rem(me - 1 + 2 * odd + n, n)

    def block(q):
        return q + even * (chunks - 1 - 2 * q)

    def sent(q):
        return q + odd * (chunks - 1 - 2 * q)

    reach = min(16, (n - 1) // 2)
    offsets = [t * o for o in range(reach, 0, -1) for t in (1, -1)]
    barrier = pltpu.get_barrier_semaphore()
    for o in offsets:
        d = lax.rem(me + o + n, n)
        pl.semaphore_signal(barrier, inc=1, device_id={"leaf": d}, device_id_type=MESH)

    own = [
        pltpu.make_async_copy(ch, cst.at[pl.ds(leaves, leaves)], own_sem.at[0]),
        pltpu.make_async_copy(lb, basis, own_sem.at[1]),
        pltpu.make_async_copy(tr, trans, own_sem.at[2]),
        pltpu.make_async_copy(cc, ccv, own_sem.at[3]),
    ]
    for copy in own:
        copy.start()

    def near_copy(q):
        return pltpu.make_async_copy(
            nb.at[pl.ds(block(q) * size, size)], nbuf.at[q], near_sem.at[q]
        )

    def coup_copy(q):
        return pltpu.make_async_copy(
            lc.at[pl.ds(block(q) * size, size)], cbuf.at[q], coup_sem.at[q]
        )

    def loop(lo, hi, body):
        def step(i, c):
            body(i)
            return c
        lax.fori_loop(lo, hi, step, 0)

    def fetch(q):
        near_copy(q).start()
        coup_copy(q).start()

    loop(0, chunks, fetch)
    pl.semaphore_wait(barrier, len(offsets))

    def remote(src, dst, send, recv, d):
        return pltpu.make_async_remote_copy(
            src_ref=src, dst_ref=dst, send_sem=send, recv_sem=recv,
            device_id={"leaf": d}, device_id_type=MESH,
        )

    def slow_c(q):
        return remote(
            ch.at[pl.ds(sent(q) * size, size)], hslow_c.at[q], sc_send.at[q], sc_recv.at[q], slow
        )

    def slow_m(q):
        return remote(mpack.at[sent(q)], hslow_m.at[q], sm_send.at[q], sm_recv.at[q], slow)

    fast_c = remote(
        ch, cst.at[pl.ds(odd * (2 * leaves), leaves)], fc_send.at[0], fc_recv.at[0], fast
    )
    fast_m = remote(mpack, hfast_m, fm_send.at[0], fm_recv.at[0], fast)

    loop(0, early, lambda q: slow_c(q).start())
    fast_c.start()
    cst[3 * leaves] = jnp.zeros(cst.shape[1:], BF16)
    for copy in own[:3]:
        copy.wait()

    left = lax.broadcasted_iota(jnp.int32, (ch.shape[1], 128), 1) < 64

    wide = 2

    def lift_step(g, lift):
        packs, pairs = [], []
        for i in range(wide * size // 2):
            leaf = g * (wide * size) + 2 * i
            b, j = g * wide + i // (size // 2), i % (size // 2)
            both = []
            for h in range(2):
                twice = jnp.concatenate([basis[leaf + h], basis[leaf + h]], axis=0)
                m = dot_t(cst[leaves + leaf + h], twice)
                mst[leaves + leaf + h] = m.astype(BF16)
                both.append(m)
            packed = jnp.where(left, both[0], both[1]).astype(BF16)
            mpack[b, j] = packed
            pair = jnp.concatenate([trans[leaf], trans[leaf + 1]], axis=1)
            tpk[b, j] = pair
            packs.append(packed)
            pairs.append(pair)
        return lift + dot_t(jnp.concatenate(packs, axis=1), jnp.concatenate(pairs, axis=1))

    def two_parts(x):
        high = x.astype(BF16)
        low = (x - high.astype(F32)).astype(BF16)
        return jnp.concatenate([high, low], axis=1)

    def folded(x):
        half = x.shape[0] // 2
        return jnp.concatenate([x[:half], x[half:]], axis=1).astype(BF16)

    def unfolded(p):
        return jnp.concatenate([p[:, :rank], p[:, rank:]], axis=0)

    rank = lb.shape[1]
    lift = lax.fori_loop(0, chunks // wide, lift_step, jnp.zeros((ch.shape[1], rank), F32))
    cmall[me] = folded(lift)
    spots = [
        remote(cmall.at[me], cmall.at[me], cl_send.at[k], cl_recv.at[k], lax.rem(me + o + n, n))
        for k, o in enumerate(offsets)
    ]
    for copy in spots:
        copy.start()
    fast_m.start()
    loop(0, 1, lambda q: slow_m(q).start())

    def spread(packed, at):
        a = packed[:, :64]
        b = packed[:, 64:]
        mst[at] = jnp.concatenate([a, a], axis=1)
        mst[at + 1] = jnp.concatenate([b, b], axis=1)

    loop(1, 2, lambda q: slow_m(q).start())
    loop(early, early + 1, lambda q: slow_c(q).start())
    fast_c.wait_recv()
    fast_m.wait_recv()
    fast_base = even * (2 * leaves)
    slow_base = odd * (2 * leaves)

    def unpack_fast(b):
        for j in range(size // 2):
            spread(hfast_m[b, j], fast_base + b * size + 2 * j)

    loop(0, chunks, unpack_fast)

    own[3].wait()

    def push(q):
        slow_m(q + 2).start()
        slow_c(q + early + 1).start()

    tail = chunks - early - 1
    loop(0, tail, push)
    loop(tail + 2, chunks, lambda q: slow_m(q).start())

    def lowered(local, b, j):
        twice = jnp.concatenate([tpk[b, j], tpk[b, j]], axis=0)
        return jnp.dot(local, twice, preferred_element_type=F32)

    def close(leaf, near, far, down):
        ll = (far + down).astype(BF16)
        far_part = jnp.dot(ll, basis[leaf], preferred_element_type=F32)
        out[leaf] = (near + far_part).astype(BF16)

    def work(q, local=None):
        slow_c(q).wait_recv()
        slow_m(q).wait_recv()
        near_copy(q).wait()
        coup_copy(q).wait()
        b = block(q)
        cst[pl.ds(slow_base + b * size, size)] = hslow_c[q]
        for j in range(size // 2):
            spread(hslow_m[q, j], slow_base + b * size + 2 * j)

        def place(index):
            return jnp.clip(lax.rem(index - first + leaves + total, total), 0, 3 * leaves - 1)

        for j in range(size // 2):
            if local is not None:
                down = lowered(local, b, j)
            for h in range(2):
                at = 2 * j + h
                leaf = b * size + at
                count = nc[leaf]
                lhs, rhs = [], []
                for s in range(slots):
                    pos = jnp.where(s < count, place(ni[s, leaf]), 3 * leaves)
                    lhs.append(cst[pos])
                    rhs.append(nbuf[q, at, s])
                near = dot_t(jnp.concatenate(lhs, axis=1), jnp.concatenate(rhs, axis=1))
                lhs, rhs = [], []
                for f in range(0, farl, 2):
                    lhs.append(
                        jnp.where(left, mst[place(fi[f, leaf])], mst[place(fi[f + 1, leaf])])
                    )
                    rhs.append(
                        jnp.concatenate([cbuf[q, at, f], cbuf[q, at, f + 1]], axis=1)
                    )
                far = dot_t(jnp.concatenate(lhs, axis=1), jnp.concatenate(rhs, axis=1))
                if local is None:
                    nsum[leaf] = near
                    fsum[leaf] = far
                else:
                    close(leaf, near, far, down[:, h * rank : h * rank + rank])

    loop(0, parted, work)
    rhs = [ccv[0, f] for f in range(ci.shape[1])]
    for k, o in enumerate(offsets):
        source = lax.rem(me - o + n, n)
        remote(
            cmall.at[source], cmall.at[source], cl_send.at[k], cl_recv.at[k], fast
        ).wait_recv()
    lhs = []
    for f in range(ci.shape[1]):
        source = jnp.clip(ci[0, f], 0, n - 1)
        lhs.append(unfolded(cmall[source]))
    local = two_parts(dot_t(jnp.concatenate(lhs, axis=1), jnp.concatenate(rhs, axis=1)))

    def settle(q):
        b = block(q)
        for j in range(size // 2):
            down = lowered(local, b, j)
            for h in range(2):
                leaf = b * size + 2 * j + h
                close(leaf, nsum[leaf], fsum[leaf], down[:, h * rank : h * rank + rank])

    loop(0, parted, settle)
    loop(parted, chunks, lambda q: work(q, local))

    def finish(q):
        slow_c(q).wait_send()
        slow_m(q).wait_send()

    loop(0, chunks, finish)
    fast_c.wait_send()
    fast_m.wait_send()
    for copy in spots:
        copy.wait_send()


def shards(n, charges, near_blocks, near_index, near_count, leaf_basis, leaf_coupling,
           far_index, transfer, cluster_coupling, cluster_index):
    leaves, rhs, points = charges.shape
    rank = leaf_basis.shape[1]
    size = 4
    chunks = leaves // size
    early = 2
    reach = min(16, (n - 1) // 2)
    hbm = pl.BlockSpec(memory_space=pl.ANY)
    smem = pl.BlockSpec(memory_space=pltpu.SMEM)
    dma = pltpu.SemaphoreType.DMA
    packed = (chunks, size // 2, rhs, 2 * rank)
    return pl.pallas_call(
        functools.partial(kernel, n, chunks, size, early, 0),
        out_shape=pltpu.VMEM(charges.shape, BF16),
        in_specs=[hbm, hbm, smem, smem, hbm, hbm, smem, hbm, hbm, smem],
        out_specs=pl.BlockSpec(memory_space=pltpu.VMEM),
        scratch_shapes=[
            pltpu.VMEM((3 * leaves + 1, rhs, points), BF16),
            pltpu.VMEM((3 * leaves, rhs, 2 * rank), BF16),
            pltpu.VMEM((chunks, size, rhs, points), BF16),
            pltpu.VMEM(packed, BF16),
            pltpu.VMEM(packed, BF16),
            pltpu.VMEM(packed, BF16),
            pltpu.VMEM((chunks, size // 2, rank, 2 * rank), BF16),
            pltpu.VMEM(leaf_basis.shape, BF16),
            pltpu.VMEM(transfer.shape, BF16),
            pltpu.VMEM(cluster_coupling.shape, BF16),
            pltpu.VMEM((n, rhs // 2, 2 * rank), BF16),
            pltpu.VMEM((chunks, size) + near_blocks.shape[1:], BF16),
            pltpu.VMEM((chunks, size) + leaf_coupling.shape[1:], BF16),
            pltpu.VMEM(charges.shape, F32),
            pltpu.VMEM((leaves, rhs, rank), F32),
            dma((1,)), dma((1,)), dma((1,)), dma((1,)),
            dma((chunks,)), dma((chunks,)), dma((chunks,)), dma((chunks,)),
            dma((2 * reach,)), dma((2 * reach,)),
            dma((4,)), dma((chunks,)), dma((chunks,)),
        ],
        compiler_params=pltpu.CompilerParams(
            collective_id=0, has_side_effects=True, vmem_limit_bytes=60 * 1024 * 1024
        ),
    )(charges, near_blocks, near_index.T, near_count, leaf_basis, leaf_coupling,
      far_index.T, transfer, cluster_coupling, cluster_index)


def solution(mesh):
    three = P(("parts", "leaf"), None, None)
    four = P(("parts", "leaf"), None, None, None)
    two = P(("parts", "leaf"), None)
    placed = (three, four, two, P(("parts", "leaf")), three, four, two, three, four, two)
    return jax.shard_map(
        functools.partial(shards, mesh.shape["leaf"]),
        mesh=mesh,
        in_specs=placed,
        out_specs=three,
        check_vma=False,
    )
```

time: 32.7 us -> 29.6 us (0.905)
  Pallas kernels: 30.6 us -> 28.3 us
  local copies, waits for them, and re-layouts: 1.87 us -> 0.8 us
    pallas_call x1, Pallas kernels: 30.6 us -> 28.3 us  [shards(): pl.pallas_call(functools.partial(kernel, n, chunks, size, early, 0), out_...]
    unnamed x1, local copies, waits for them, and re-layouts: 1.87 us -> 0.8 us
where the time goes in v2:
time: 29.6 us; the launch traced here: 29.2 us
  Pallas kernels  28.3 us (96%)
  local copies, waits for them, and re-layouts  0.8 us (3%)
    pallas_call x1, Pallas kernels, shards(): pl.pallas_call(functools.partial(kernel, n, chunks, size, early, 0), out_...  28.3 us
    unnamed x1, local copies, waits for them, and re-layouts  0.8 us

profile of v2, /device:TPU:1, one launch (start us, length us, event | category | flops | bytes accessed | tf_op | source)
XLA Modules:
  0.0 29.2 jit_solution(4399243462997204257)
XLA Ops:
  0.0 28.3 %shard_map.100 = bf16[32,64,128]{2,1,0:T(8,128)(2,1)S(1)} custom-call(bf16[32,64,128]{2,1,0:T(8,128)(2,1)} %ch.1, bf16[32,8,128,128]{3,2,1,0:T(8,128)(2,1)} %nb.1, s32[8,32]{1,0:T(8,128)} %bitcast.2, s32[32]{0:T(128)} %nc.1, bf16[32,64,128]{2,1,0:T(8,128)(2,1)} %lb.1, bf16[32,8,64,64]{3,2,1,0:T(8,128)(2,1)} %lc.1, s32[8,32]{1,0:T(8,128)} %bitcast.3, ...), custom_call_target="tpu_custom_call" | custom-call | tf_op jit(solution)/shard_map/pallas_call | solution.py:280
  28.4 0.8 %copy.12 = bf16[32,64,128]{2,1,0:T(8,128)(2,1)} copy(bf16[32,64,128]{2,1,0:T(8,128)(2,1)S(1)} %shard_map.100) | data formatting | bytes 1048576

commit v3 on v2

--- a/solution.py
+++ b/solution.py
@@ -106,7 +106,7 @@
 
     left = lax.broadcasted_iota(jnp.int32, (ch.shape[1], 128), 1) < 64
 
-    wide = 2
+    wide = 4
 
     def lift_step(g, lift):
         packs, pairs = [], []
@@ -271,7 +271,7 @@
     rank = leaf_basis.shape[1]
     size = 4
     chunks = leaves // size
-    early = 2
+    early = 1
     reach = min(16, (n - 1) // 2)
     hbm = pl.BlockSpec(memory_space=pl.ANY)
     smem = pl.BlockSpec(memory_space=pltpu.SMEM)

time: 29.6 us -> 29 us (0.980)
  Pallas kernels: 28.3 us -> 28 us
    pallas_call x1, Pallas kernels: 28.3 us -> 28 us  [shards(): pl.pallas_call(functools.partial(kernel, n, chunks, size, early, 0), out_...]
where the time goes in v3:
time: 29 us; the launch traced here: 28.8 us
  Pallas kernels  28 us (97%)
  local copies, waits for them, and re-layouts  0.8 us (3%)
    pallas_call x1, Pallas kernels, shards(): pl.pallas_call(functools.partial(kernel, n, chunks, size, early, 0), out_...  28 us
    unnamed x1, local copies, waits for them, and re-layouts  0.8 us

profile of v3, /device:TPU:1, one launch (start us, length us, event | category | flops | bytes accessed | tf_op | source)
XLA Modules:
  0.0 28.8 jit_solution(2799370988335133336)
XLA Ops:
  0.0 28.0 %shard_map.100 = bf16[32,64,128]{2,1,0:T(8,128)(2,1)S(1)} custom-call(bf16[32,64,128]{2,1,0:T(8,128)(2,1)} %ch.1, bf16[32,8,128,128]{3,2,1,0:T(8,128)(2,1)} %nb.1, s32[8,32]{1,0:T(8,128)} %bitcast.2, s32[32]{0:T(128)} %nc.1, bf16[32,64,128]{2,1,0:T(8,128)(2,1)} %lb.1, bf16[32,8,64,64]{3,2,1,0:T(8,128)(2,1)} %lc.1, s32[8,32]{1,0:T(8,128)} %bitcast.3, ...), custom_call_target="tpu_custom_call" | custom-call | tf_op jit(solution)/shard_map/pallas_call | solution.py:280
  28.0 0.8 %copy.12 = bf16[32,64,128]{2,1,0:T(8,128)(2,1)} copy(bf16[32,64,128]{2,1,0:T(8,128)(2,1)S(1)} %shard_map.100) | data formatting | bytes 1048576
